TPU v7x, 256 devices: a whole 4x4x8 slice. The times are simulated.
256 devices in a mesh: tok: 32 (over y, x, core), lat: 8 (over z).
Axes of the slice: x: 4, y: 4, z: 8, core: 2. Of those that a mesh axis runs over, the one named last changes fastest.
Arguments:
- captured: bfloat16 [4096, 16384], P(None, 'tok'), may hold values from -6 to 6
- enc_weight: bfloat16 [16384, 16384], P('tok', 'lat'), may hold values from -0.046875 to 0.046875
- enc_bias: float32 [16384], P('lat'), may hold values from -3 to 3
- dec_weight: bfloat16 [16384, 16384], P('lat', 'tok'), may hold values from -0.125 to 0.125
- dec_bias: float32 [16384], P('tok'), may hold values from -1.5 to 1.5
- block_ids: int32 [32, 8, 2], P(None, 'lat'), may hold values from 0 to 15, as said below
- block_counts: int32 [32, 8], P(None, 'lat'), may hold values from 1 to 2, as said below
Outputs:
- enc_grad: bfloat16 [16384, 16384], P('tok', 'lat')
- dec_grad: bfloat16 [16384, 16384], P('lat', 'tok')
Inputs may be any that keep to these rules, and one draw needn't show every extreme that they name: block_ids[b, s, k] numbers a latent block within latent shard s; the 2 entries of one token block and shard are distinct, and those with k >= block_counts[b, s] are inactive slots. block_counts[b, s] is how many leading slots of block_ids[b, s] are active; some entry equals 2 in every draw.
All inputs are finite; a program needn't handle non-finite values.
Results may differ from a plain program's by a relative error of at most 0.02.
Values may be sent and summed in bfloat16 or wider, within the bound.
No kernel may reach another device: no remote copies, remote signals or barrier semaphores. Data moves between devices by JAX's collectives and lax.ppermute only.
A program may use at most 128 MiB of HBM per device.

v0:
```python
import jax
import jax.numpy as jnp
from jax import lax
from jax.sharding import PartitionSpec as P

TB = 128
LB = 128
KS = 2


SCALE_ERR = 0.0625
PENALTY = 0.05


def local(captured, enc_weight, enc_bias, dec_weight, dec_bias, block_ids, block_counts):
    features = captured.shape[1]
    lat_dev = enc_weight.shape[1]
    lat_blocks = lat_dev // LB
    all_blocks = captured.shape[0] // TB
    own_blocks = all_blocks // lax.axis_size("tok")
    first_block = lax.axis_index("tok") * own_blocks
    ids_all = block_ids.reshape(all_blocks, KS)
    counts_all = block_counts.reshape(all_blocks)
    enc_cube = enc_weight.reshape(features, lat_blocks, LB)
    dec_cube = dec_weight.reshape(lat_blocks, LB, features)
    acts_blocks = captured.reshape(all_blocks, TB, features)
    selector = (
        ids_all[:, :, None] == jnp.arange(lat_blocks, dtype=jnp.int32)[None, None, :]
    ).astype(jnp.float32)
    block_rows = acts_blocks
    chosen = ids_all
    weight_tiles = jnp.take(enc_cube, chosen, axis=1)
    pre_sum = lax.psum_scatter(
        jnp.einsum(
            "btf,fbkc->bktc", block_rows, weight_tiles, preferred_element_type=jnp.float32
        ).astype(jnp.bfloat16),
        "tok",
        scatter_dimension=0,
        tiled=True,
    ).astype(jnp.float32)
    own_ids = lax.dynamic_slice_in_dim(ids_all, first_block, own_blocks, 0)
    own_counts = lax.dynamic_slice_in_dim(counts_all, first_block, own_blocks, 0)
    bias_tiles = jnp.take(enc_bias.reshape(lat_blocks, LB), own_ids, axis=0)
    live_slots = (jnp.arange(KS, dtype=jnp.int32)[None, :] < own_counts[:, None]).astype(
        jnp.float32
    )
    pre_act = pre_sum + bias_tiles[:, :, None, :]
    codes_own = (jax.nn.softplus(pre_act) * live_slots[:, :, None, None]).astype(jnp.bfloat16)
    codes_all = lax.all_gather(codes_own, "tok", axis=0, tiled=True)
    dec_tiles = jnp.take(dec_cube, ids_all, axis=0)
    partial_value = jnp.einsum(
        "bktc,bkcf->btf", codes_all, dec_tiles, preferred_element_type=jnp.float32
    )
    partial_value = lax.optimization_barrier(partial_value.astype(jnp.bfloat16)).astype(jnp.float32)
    rebuilt = lax.psum(
        partial_value.reshape(all_blocks * TB, features).astype(jnp.bfloat16), "lat"
    ).astype(jnp.float32)
    err_grad = SCALE_ERR * (rebuilt + dec_bias[None, :] - captured.astype(jnp.float32))
    err_half = err_grad.astype(jnp.bfloat16).reshape(all_blocks, TB, features)
    tile_grads = jnp.einsum(
        "bktc,btf->bkcf", codes_all, err_half, preferred_element_type=jnp.float32
    )
    dec_total = jnp.einsum("bkj,bkcf->jcf", selector, tile_grads, precision=lax.Precision.HIGHEST)
    dec_grad = dec_total.reshape(lat_dev, features).astype(jnp.bfloat16)
    weight_tiles = dec_tiles
    dcode_all = lax.psum(
        jnp.einsum(
            "btf,bkcf->bktc", err_half, weight_tiles, preferred_element_type=jnp.float32
        ).astype(jnp.bfloat16),
        "tok",
    ).astype(jnp.float32)
    dpre_all = ((dcode_all + PENALTY) * (1.0 - jnp.exp(-codes_all.astype(jnp.float32)))).astype(
        jnp.bfloat16
    )
    block_rows = acts_blocks
    chosen = selector
    products = jnp.einsum(
        "btf,bktc->bkfc", block_rows, dpre_all, preferred_element_type=jnp.float32
    )
    enc_total = jnp.einsum("bkj,bkfc->fjc", chosen, products, precision=lax.Precision.HIGHEST)
    enc_grad = enc_total.reshape(features, lat_dev).astype(jnp.bfloat16)
    return (enc_grad, dec_grad)


def solution(mesh):
    in_specs = (
        P(None, "tok"),
        P("tok", "lat"),
        P("lat"),
        P("lat", "tok"),
        P("tok"),
        P(None, "lat", None),
        P(None, "lat"),
    )
    out_specs = (P("tok", "lat"), P("lat", "tok"))
    return jax.shard_map(local, mesh=mesh, in_specs=in_specs, out_specs=out_specs, check_vma=False)
```

profile of v0, /device:TPU:6, one launch (start us, length us, event | category | flops | bytes accessed | tf_op | source)
XLA Modules:
  0.0 482.7 jit_solution(4434560896824483886)
XLA Ops:
  7.2 0.0 copy-start
  7.2 0.0 reduce-scatter.2.cloned.1.call-start
  7.2 0.8 compare_and_fusion.1
  8.1 0.7 compare_select_fusion.1
  8.7 0.1 copy.30
  8.8 0.1 copy.31
  8.9 0.1 reshape.177
  9.0 3.9 copy.33
  13.0 3.9 copy.34
  16.9 7.1 %gather_fusion.1 = bf16[64,512,128]{2,1,0:T(8,128)(2,1)} fusion(bf16[512,16,128]{2,0,1:T(8,128)(2,1)} %copy.34, s32[1024]{0:T(1024)S(1)} %pad_clamp_fusion.1), kind=kCustom, calls=%fused_computation.1 | custom fusion | bytes 16777472 | tf_op jit(solution)/shard_map/jit(_take)/gather | solution.py:32
  24.0 11.9 %copy.35 = bf16[32,2,512,128]{2,3,1,0:T(8,128)(2,1)} copy(bf16[32,2,512,128]{3,2,1,0:T(8,128)(2,1)} %bitcast.67) | data formatting | bytes 16777216 | tf_op jit(solution)/shard_map/jit(_take)/gather | solution.py:32
  35.9 8.3 %convert_bitcast_fusion.1 = bf16[32,2,128,128]{2,3,1,0:T(8,128)(2,1)} fusion(bf16[32,128,512,1]{2,1,3,0:T(8,128)(2,1)} %bitcast.68, bf16[32,2,512,128]{2,3,1,0:T(8,128)(2,1)} %copy.35, pred[32,2]{1,0:T(8,128)(4,1)S(1)} %copy.30), kind=kOutput, calls=%fused_computation.25 | convolution fusion | flops 1078984704 | bytes 14680128 | tf_op jit(solution)/shard_map/btf,fbkc->bktc/dot_general | solution.py:34
  44.2 0.0 reduce-scatter.2.cloned.1.call-update
  44.2 0.0 all-gather.2.cloned.1.call-start
  44.3 0.0 copy-done.5
  44.3 0.2 dynamic-slice_reduce_fusion
  44.5 0.6 constant_dynamic-slice_fusion
  45.1 0.0 copy-done.6
  45.1 0.6 gather_fusion.2
  45.7 0.6 compare_convert_fusion
  46.3 0.1 broadcast_select_fusion.7
  46.4 87.1 %reduce-scatter.2.cloned.1.call-done = bf16[1,2,128,128]{2,3,1,0:T(8,128)(2,1)} async-done(((bf16[32,2,128,128]{2,3,1,0:T(8,128)(2,1)}), bf16[1,2,128,128]{2,3,1,0:T(8,128)(2,1)}) %reduce-scatter.2.cloned.1.call-update) | async-done | bytes 65552 | tf_op jit(solution)/shard_map/reduce_scatter | solution.py:33
  133.5 1.0 fusion.18
  134.5 0.7 copy.36
  135.3 0.0 all-gather.2.cloned.1.call-update
  135.3 0.0 all-reduce.3.cloned.1.call-start
  135.3 5.5 %gather_fusion = bf16[64,128,512]{2,1,0:T(8,128)(2,1)} fusion(bf16[16,128,512]{2,1,0:T(8,128)(2,1)S(1)} %bitcast.64, s32[1024]{0:T(1024)S(1)} %pad_clamp_fusion.1), kind=kCustom, calls=%fused_computation | custom fusion | bytes 16777472 | tf_op jit(solution)/shard_map/jit(_take)/gather | solution.py:50
  140.9 43.9 %all-gather.2.cloned.1.call-done = bf16[32,2,128,128]{3,2,1,0:T(8,128)(2,1)} async-done(((bf16[1,2,128,128]{3,2,1,0:T(8,128)(2,1)}), bf16[32,2,128,128]{3,2,1,0:T(8,128)(2,1)}) %all-gather.2.cloned.1.call-update) | async-done | bytes 2097168 | tf_op jit(solution)/shard_map/all_gather | solution.py:49
  184.8 7.7 %bitcast_convert_fusion = bf16[32,128,512]{2,1,0:T(8,128)(2,1)} fusion(bf16[32,2,128,128]{3,2,1,0:T(8,128)(2,1)} %all-gather.2.cloned.1.call-done, bf16[32,2,128,512]{3,2,1,0:T(8,128)(2,1)} %bitcast.70, pred[32,2]{1,0:T(8,128)(4,1)S(1)} %copy.30), kind=kOutput, calls=%fused_computation.6 | convolution fusion | flops 1080033280 | bytes 14680128 | tf_op jit(solution)/shard_map/bktc,bkcf->btf/dot_general | solution.py:51
  192.4 0.0 all-reduce.3.cloned.1.call-update
  192.5 0.2 all-reduce.5.cloned.1.call-start
  192.7 1.3 copy-done.3
  194.0 2.9 copy.37
  196.9 104.5 %all-reduce.3.cloned.1.call-done = bf16[4096,512]{1,0:T(8,128)(2,1)} async-done(((bf16[4096,512]{1,0:T(8,128)(2,1)}), bf16[4096,512]{1,0:T(8,128)(2,1)}) %all-reduce.3.cloned.1.call-update) | async-done | bytes 4194320 | tf_op jit(solution)/shard_map/psum | solution.py:55
  301.4 0.0 copy-done.7
  301.4 5.0 %multiply_convert_fusion = bf16[4096,512]{1,0:T(8,128)(2,1)S(1)} fusion(bf16[4096,512]{1,0:T(8,128)(2,1)} %param.7, bf16[4096,512]{1,0:T(8,128)(2,1)} %all-reduce.3.cloned.1.call-done, f32[512]{0:T(512)S(1)} %copy-done.7), kind=kLoop, calls=%fused_computation.10 | loop fusion | flops 12582912 | bytes 12584960 | tf_op jit(solution)/shard_map/convert_element_type | solution.py:59
  306.4 2.0 copy-done.2
  308.4 7.1 %convert_bitcast_fusion = bf16[32,2,128,128]{2,3,1,0:T(8,128)(2,1)} fusion(bf16[32,128,512,1]{2,1,3,0:T(8,128)(2,1)S(1)} %bitcast.65, bf16[32,2,128,512]{3,2,1,0:T(8,128)(2,1)} %bitcast.71, pred[32,2]{1,0:T(8,128)(4,1)S(1)} %copy.30), kind=kOutput, calls=%fused_computation.24 | convolution fusion | flops 1078984704 | bytes 14680128 | tf_op jit(solution)/shard_map/btf,bkcf->bktc/dot_general | solution.py:67
  315.5 0.0 all-reduce.5.cloned.1.call-update
  315.5 4.6 fusion.30
  320.1 12.1 %bitcast_convert_fusion.1 = bf16[16,128,512]{2,0,1:T(8,128)(2,1)S(1)} fusion(f32[32,2,128,512]{3,2,1,0:T(8,128)S(1)} %fusion.30, s32[32,2]{0,1:T(2,128)S(1)} %bitcast.77), kind=kOutput, calls=%fused_computation.15 | convolution fusion | flops 806355968 | bytes 18874624 | tf_op jit(solution)/shard_map/bkj,bkcf->jcf/dot_general | solution.py:63
  332.2 0.0 copy-start.4
  332.2 2.5 copy.41
  334.7 98.1 %all-reduce.5.cloned.1.call-done = bf16[32,2,128,128]{2,3,1,0:T(8,128)(2,1)} async-done(((bf16[32,2,128,128]{2,3,1,0:T(8,128)(2,1)}), bf16[32,2,128,128]{2,3,1,0:T(8,128)(2,1)}) %all-reduce.5.cloned.1.call-update) | async-done | bytes 2097168 | tf_op jit(solution)/shard_map/psum | solution.py:66
  432.8 10.9 %convolution_bitcast_fusion = f32[32,2,512,128]{2,3,1,0:T(8,128)} fusion(bf16[32,128,512,1]{2,1,3,0:T(8,128)(2,1)} %bitcast.69, bf16[32,2,128,128]{2,3,1,0:T(8,128)(2,1)S(1)} %copy-done.4, bf16[32,2,128,128]{2,3,1,0:T(8,128)(2,1)} %all-reduce.5.cloned.1.call-done), kind=kOutput, calls=%fused_computation.5 | convolution fusion | flops 1081081856 | bytes 25165824 | tf_op jit(solution)/shard_map/btf,bktc->bkfc/dot_general | solution.py:77
  443.7 20.2 %copy.38 = f32[32,2,512,128]{3,0,1,2:T(8,128)} copy(f32[32,2,512,128]{2,3,1,0:T(8,128)} %convolution_bitcast_fusion) | data formatting | bytes 33554432 | tf_op jit(solution)/shard_map/btf,bktc->bkfc/transpose | solution.py:77
  463.9 10.4 %bitcast_convert_fusion.2 = bf16[512,128,16]{1,2,0:T(8,128)(2,1)S(1)} fusion(f32[32,2,512,128]{3,0,1,2:T(8,128)} %copy.38, s32[32,2]{0,1:T(2,128)S(1)} %bitcast.78), kind=kOutput, calls=%fused_computation.16 | convolution fusion | flops 806355968 | bytes 18874624 | tf_op jit(solution)/shard_map/bkj,bkfc->fjc/dot_general | solution.py:80
  474.3 1.9 copy.54
  (15 shorter events, 0.0 us)
Async XLA Ops:
  7.2 128.2 %copy-start = (bf16[2048,512]{1,0:T(8,128)(2,1)S(1)}, bf16[2048,512]{1,0:T(8,128)(2,1)}, u32[]{:S(2)}) copy-start(bf16[2048,512]{1,0:T(8,128)(2,1)} %param.10) | copy-start | bytes 6291460
  7.2 126.3 %reduce-scatter.2.cloned.1.call-start = ((), (), s32[]{:S(2)}) async-start(), calls=%async_computation.1 | async-start | bytes 2162688 | tf_op jit(solution)/shard_map/reduce_scatter | solution.py:33
  35.9 8.4 %copy-start.5 = (s32[32,1,2]{0,2,1:T(2,128)S(1)}, s32[32,1,2]{0,2,1:T(2,128)}, u32[]{:S(2)}) copy-start(s32[32,1,2]{0,2,1:T(2,128)} %param.12) | copy-start | bytes 772
  35.9 8.6 %copy-start.8 = (s32[32,1]{0,1:T(1,128)S(1)}, s32[32,1]{0,1:T(1,128)}, u32[]{:S(2)}) copy-start(s32[32,1]{0,1:T(1,128)} %param.13) | copy-start | bytes 388
  35.9 9.2 %copy-start.6 = (f32[2048]{0:T(1024)S(1)}, f32[2048]{0:T(1024)}, u32[]{:S(2)}) copy-start(f32[2048]{0:T(1024)} %param.9) | copy-start | bytes 24580
  44.2 140.5 %all-gather.2.cloned.1.call-start = ((), (), s32[]{:S(2)}) async-start(), calls=%async_computation.2 | async-start | bytes 2162688 | tf_op jit(solution)/shard_map/all_gather | solution.py:49
  135.3 166.1 %all-reduce.3.cloned.1.call-start = ((), (), s32[]{:S(2)}) async-start(), calls=%async_computation.3 | async-start | bytes 8388608 | tf_op jit(solution)/shard_map/psum | solution.py:55
  192.4 1.6 copy-start.3
  192.4 108.9 %copy-start.7 = (f32[512]{0:T(512)S(1)}, f32[512]{0:T(512)}, u32[]{:S(2)}) copy-start(f32[512]{0:T(512)} %param.11) | copy-start | bytes 6148
  192.5 240.3 %all-reduce.5.cloned.1.call-start = ((), (), s32[]{:S(2)}) async-start(), calls=%async_computation.4 | async-start | bytes 4194304 | tf_op jit(solution)/shard_map/psum | solution.py:66
  306.4 2.0 copy-start.2
  332.2 100.6 %copy-start.4 = (bf16[32,2,128,128]{2,3,1,0:T(8,128)(2,1)S(1)}, bf16[32,2,128,128]{2,3,1,0:T(8,128)(2,1)}, u32[]{:S(2)}) copy-start(bf16[32,2,128,128]{2,3,1,0:T(8,128)(2,1)} %copy.37) | copy-start | bytes 6291460
  463.9 12.3 %copy-start.1 = (bf16[2048,512]{1,0:T(8,128)(2,1)S(1)}, bf16[2048,512]{1,0:T(8,128)(2,1)}, u32[]{:S(2)}) copy-start(bf16[2048,512]{1,0:T(8,128)(2,1)} %param.10) | copy-start | bytes 6291460
Sparse Core Ops, SparseCore 0:
  44.4 89.1 reduce-scatter.1
  136.6 48.0 all-gather.1
  192.6 108.7 all-reduce.2
  315.6 117.0 all-reduce.4
where the time goes:
time: 484 us; the launch traced here: 483 us
  waiting for transfers between devices  334 us (69%)
  local copies, waits for them, and re-layouts  65.5 us (14%)
  matrix products  61 us (13%)
  between operations  13.9 us (3%)
  other arithmetic  8.29 us (2%)
    psum x1, waiting for transfers between devices, local(): lax.psum(partial_value.reshape(all_blocks * TB, features).astype(jnp.bflo...  104 us
    psum x1, waiting for transfers between devices, local(): lax.psum(jnp.einsum('btf,bkcf->bktc', err_half, weight_tiles, preferred_e...  98.1 us
    reduce_scatter x1, waiting for transfers between devices, local(): lax.psum_scatter(jnp.einsum('btf,fbkc->bktc', block_rows, weight_tiles, p...  87.1 us
    all_gather x1, waiting for transfers between devices, local(): codes_all = lax.all_gather(codes_own, 'tok', axis=0, tiled=True)  43.9 us
    transpose x1, local copies, waits for them, and re-layouts, local(): jnp.einsum('btf,bktc->bkfc', block_rows, dpre_all, preferred_element_type...  20.2 us
    gather x2, local copies, waits for them, and re-layouts, local(): weight_tiles = jnp.take(enc_cube, chosen, axis=1)  19 us
    dot_general x1, matrix products, local(): jnp.einsum('bkj,bkcf->jcf', selector, tile_grads, precision=lax.Precision...  12.1 us
    dot_general x1, matrix products, local(): jnp.einsum('btf,bktc->bkfc', block_rows, dpre_all, preferred_element_type...  10.9 us
  transfers between devices with their start and end apart: 4, of which 4 were waited for; matrix products, arithmetic and copies ran while one was open for 6% of the time, Pallas kernels for 0%

commit v1 on v0

v1 whole, which is shorter than its diff:
```python
import functools

import jax
import jax.numpy as jnp
from jax import lax
from jax.experimental import pallas as pl
from jax.experimental.pallas import tpu as pltpu
from jax.sharding import Mesh, PartitionSpec as P

TB = 128
LB = 128
KS = 2
NTB = 32
NY, NX, NC, NZ = 4, 4, 2, 8
CHIPS = NY * NX
GROUPS = 1
NB = NTB // GROUPS
BPC = NB // CHIPS
BPZ = NB // NZ
HALF = BPZ // 2 * TB

SCALE_ERR = 0.0625
PENALTY = 0.05

BF = jnp.bfloat16
F32 = jnp.float32
VMEM_LIMIT = 40 * 1024 * 1024

COUNTS, CORE, CHIP, ZPOS = NTB * KS, NTB * KS + NTB, NTB * KS + NTB + 1, NTB * KS + NTB + 2

SMEM = pl.BlockSpec(memory_space=pltpu.SMEM)
VMEM = pl.BlockSpec(memory_space=pltpu.VMEM)


def params():
    return pltpu.CompilerParams(vmem_limit_bytes=VMEM_LIMIT)


def cost(flops, nbytes):
    return pl.CostEstimate(flops=flops, bytes_accessed=nbytes, transcendentals=0)


def rows_of(block):
    return pl.ds(pl.multiple_of(block * TB, TB), TB)


def pair_of(meta, gid):
    core = meta[CORE]
    return meta[KS * gid + core], meta[KS * gid + 1 - core]


def enc_kernel(first, step_blocks, meta, cap, enc, mine, theirs):
    base = first + pl.program_id(0) * step_blocks

    def body(b, carry):
        ia, ib = pair_of(meta, base + b)
        w = jnp.concatenate([enc[:, rows_of(ia)], enc[:, rows_of(ib)]], axis=1)
        out = jnp.dot(cap[rows_of(b), :], w, preferred_element_type=F32).astype(BF)
        mine[rows_of(b), :] = out[:, :LB]
        theirs[rows_of(b), :] = out[:, LB:]
        return carry

    lax.fori_loop(0, step_blocks, body, 0, unroll=2)


def encode(group, meta, captured, enc):
    steps = 4
    sb = NB // steps
    feats = captured.shape[1]
    out = jax.ShapeDtypeStruct((NB * TB, LB), BF)
    spec = pl.BlockSpec((sb * TB, LB), lambda i: (i, 0))
    return pl.pallas_call(
        functools.partial(enc_kernel, group * NB, sb),
        grid=(steps,),
        in_specs=[
            SMEM,
            pl.BlockSpec((sb * TB, feats), lambda i: (group * steps + i, 0)),
            pl.BlockSpec(enc.shape, lambda i: (0, 0)),
        ],
        out_specs=[spec, spec],
        out_shape=[out, out],
        compiler_params=params(),
        cost_estimate=cost(2 * NB * TB * feats * KS * LB, NB * TB * (feats + 256) * 2 + enc.size * 2),
        name="encode",
    )(meta, captured, enc)


def codes_kernel(first, meta, terms, bias, copies, own):
    for q in range(BPC):
        gid = first + meta[CHIP] * BPC + q
        core = meta[CORE]
        row = bias[pl.ds(meta[KS * gid + core], 1), :]
        v = jnp.sum(terms[:, q * TB : (q + 1) * TB, :].astype(F32), axis=0) + row
        soft = jnp.maximum(v, 0.0) + jnp.log1p(jnp.exp(-jnp.abs(v)))
        code = jnp.where(core < meta[COUNTS + gid], soft, 0.0).astype(BF)
        own[q * TB : (q + 1) * TB, :] = code
        for chip in range(CHIPS):
            copies[chip, q * TB : (q + 1) * TB, :] = code


def make_codes(group, meta, terms, bias):
    return pl.pallas_call(
        functools.partial(codes_kernel, group * NB),
        in_specs=[SMEM, VMEM, VMEM],
        out_specs=[VMEM, VMEM],
        out_shape=[jax.ShapeDtypeStruct(terms.shape, BF), jax.ShapeDtypeStruct(terms.shape[1:], BF)],
        compiler_params=params(),
        cost_estimate=cost(20 * terms.size, 4 * terms.size),
        name="codes",
    )(meta, terms, bias)


def dpre_kernel(terms, own, copies):
    total = jnp.sum(terms[...].astype(F32), axis=0)
    grad = ((total + PENALTY) * (1.0 - jnp.exp(-own[...].astype(F32)))).astype(BF)
    for chip in range(CHIPS):
        copies[chip] = grad


def make_dpre(terms, own):
    return pl.pallas_call(
        dpre_kernel,
        in_specs=[VMEM, VMEM],
        out_specs=VMEM,
        out_shape=jax.ShapeDtypeStruct(terms.shape, BF),
        compiler_params=params(),
        cost_estimate=cost(20 * terms.size, 4 * terms.size),
        name="dpre",
    )(terms, own)


ORDER = (0, 1, 7, 2, 6, 3, 5, 4)


def piece_shapes(feats):
    full = jax.ShapeDtypeStruct((BPZ * TB, feats), BF)
    half = jax.ShapeDtypeStruct((HALF, feats), BF)
    return [full] * 7 + [half, half]


def piece_at(pieces, slot, j):
    if slot < 7:
        return pieces[slot], j * TB
    if j * TB < HALF:
        return pieces[7], j * TB
    return pieces[8], j * TB - HALF


def part_kernel(first, meta, mine, other, dec, *pieces):
    for slot, ahead in enumerate(ORDER):
        chunk = lax.rem(meta[ZPOS] + ahead, NZ)
        for j in range(BPZ):
            b = chunk * BPZ + j
            ia, ib = pair_of(meta, first + b)
            codes = jnp.concatenate([mine[rows_of(b), :], other[rows_of(b), :]], axis=1)
            w = jnp.concatenate([dec[rows_of(ia), :], dec[rows_of(ib), :]], axis=0)
            piece, row = piece_at(pieces, slot, j)
            piece[row : row + TB, :] = jnp.dot(codes, w, preferred_element_type=F32).astype(BF)


def make_parts(group, meta, mine, other, dec):
    feats = dec.shape[1]
    shapes = piece_shapes(feats)
    return pl.pallas_call(
        functools.partial(part_kernel, group * NB),
        in_specs=[SMEM, VMEM, VMEM, VMEM],
        out_specs=[VMEM] * 9,
        out_shape=shapes,
        compiler_params=params(),
        cost_estimate=cost(2 * NB * TB * feats * KS * LB, NB * TB * (feats + 256) * 2 + dec.size * 2),
        name="parts",
    )(meta, mine, other, dec)


def add_kernel(n, *refs):
    for i in range(n):
        a, b, o = refs[2 * i], refs[2 * i + 1], refs[2 * n + i]
        o[...] = (a[...].astype(F32) + b[...].astype(F32)).astype(BF)


def add_first_kernel(pa, ra, pb, rb, oa, ob):
    oa[:HALF, :] = (pa[:HALF, :].astype(F32) + ra[...].astype(F32)).astype(BF)
    oa[HALF:, :] = pa[HALF:, :]
    ob[:HALF, :] = pb[:HALF, :]
    ob[HALF:, :] = (pb[HALF:, :].astype(F32) + rb[...].astype(F32)).astype(BF)


def add_both(kernel, pa, ra, pb, rb):
    out = jax.ShapeDtypeStruct(pa.shape, BF)
    return pl.pallas_call(
        kernel,
        in_specs=[VMEM] * 4,
        out_specs=[VMEM] * 2,
        out_shape=[out, out],
        compiler_params=params(),
        cost_estimate=cost(2 * pa.size, 12 * pa.size),
        name="ring_add",
    )(pa, ra, pb, rb)


def delta_kernel(meta, part, ra, rb, bias, cap, out):
    rec = part[...].astype(F32) + ra[...].astype(F32) + rb[...].astype(F32)
    out[...] = (SCALE_ERR * (rec + bias[...] - cap[...].astype(F32))).astype(BF)


def make_delta(group, meta, part, ra, rb, bias, captured):
    feats = captured.shape[1]
    rows = BPZ * TB
    block = pl.BlockSpec((rows, feats), lambda i, meta: (0, 0))
    return pl.pallas_call(
        delta_kernel,
        grid_spec=pltpu.PrefetchScalarGridSpec(
            num_scalar_prefetch=1,
            grid=(1,),
            in_specs=[
                block,
                block,
                block,
                pl.BlockSpec((1, feats), lambda i, meta: (0, 0)),
                pl.BlockSpec((rows, feats), lambda i, meta: (group * NZ + meta[ZPOS], 0)),
            ],
            out_specs=block,
        ),
        out_shape=jax.ShapeDtypeStruct((rows, feats), BF),
        compiler_params=params(),
        cost_estimate=cost(6 * rows * feats, 10 * rows * feats),
        name="delta",
    )(meta, part, ra, rb, bias, captured)


RIGHT = [(i, (i + 1) % NZ) for i in range(NZ)]
LEFT = [(i, (i - 1) % NZ) for i in range(NZ)]
SWAP = [(0, 1), (1, 0)]


def to_right(x):
    return lax.ppermute(x, "lat", RIGHT)


def to_left(x):
    return lax.ppermute(x, "lat", LEFT)


def reduce_z(group, meta, pieces, bias, captured):
    r, l = to_right(pieces[7]), to_left(pieces[8])
    a, b = add_both(add_first_kernel, pieces[5], r, pieces[6], l)
    r, l = to_right(a), to_left(b)
    for slot in (3, 1):
        a, b = add_both(functools.partial(add_kernel, 2), pieces[slot], r, pieces[slot + 1], l)
        r, l = to_right(a), to_left(b)
    return make_delta(group, meta, pieces[0], r, l, bias, captured)


def gather_z(own):
    out = [own]
    r = l = own
    for _ in range(3):
        r, l = to_right(r), to_left(l)
        out += [l, r]
    half = own.shape[0] // 2
    return out + [to_right(r[:half]), to_left(l[half:])]


def dcodes_kernel(first, meta, dec, *refs):
    pieces, (mine, theirs) = refs[:9], refs[9:]
    for slot, ahead in enumerate(ORDER):
        chunk = lax.rem(meta[ZPOS] + ahead, NZ)
        for j in range(BPZ):
            b = chunk * BPZ + j
            ia, ib = pair_of(meta, first + b)
            w = jnp.concatenate([dec[rows_of(ia), :], dec[rows_of(ib), :]], axis=0)
            piece, row = piece_at(pieces, slot, j)
            out = lax.dot_general(
                piece[row : row + TB, :], w, (((1,), (1,)), ((), ())), preferred_element_type=F32
            ).astype(BF)
            mine[rows_of(b), :] = out[:, :LB]
            theirs[rows_of(b), :] = out[:, LB:]


def make_dcodes(group, meta, dec, pieces):
    feats = dec.shape[1]
    out = jax.ShapeDtypeStruct((NB * TB, LB), BF)
    return pl.pallas_call(
        functools.partial(dcodes_kernel, group * NB),
        in_specs=[SMEM] + [VMEM] * 10,
        out_specs=[VMEM, VMEM],
        out_shape=[out, out],
        compiler_params=params(),
        cost_estimate=cost(2 * NB * TB * feats * KS * LB, NB * TB * (feats + 256) * 2 + dec.size * 2),
        name="dcodes",
    )(meta, dec, *pieces)


def dec_grad_kernel(meta, *refs):
    out, acc = refs[-2:]
    acc[...] = jnp.zeros_like(acc)
    for g in range(GROUPS):
        mine, other = refs[11 * g : 11 * g + 2]
        pieces = refs[11 * g + 2 : 11 * g + 11]
        for slot, ahead in enumerate(ORDER):
            chunk = lax.rem(meta[ZPOS] + ahead, NZ)
            for j in range(BPZ):
                b = chunk * BPZ + j
                ia, ib = pair_of(meta, g * NB + b)
                codes = jnp.concatenate([mine[rows_of(b), :], other[rows_of(b), :]], axis=1)
                piece, row = piece_at(pieces, slot, j)
                prod = lax.dot_general(
                    codes, piece[row : row + TB, :], (((0,), (0,)), ((), ())), preferred_element_type=F32
                )
                acc[rows_of(ia), :] += prod[:LB]
                acc[rows_of(ib), :] += prod[LB:]
    out[...] = acc[...].astype(BF)


def make_dec_grad(meta, shape, groups):
    args = [a for mine, other, pieces in groups for a in (mine, other, *pieces)]
    return pl.pallas_call(
        dec_grad_kernel,
        in_specs=[SMEM] + [VMEM] * len(args),
        out_specs=VMEM,
        out_shape=jax.ShapeDtypeStruct(shape, BF),
        scratch_shapes=[pltpu.VMEM(shape, F32)],
        compiler_params=params(),
        cost_estimate=cost(2 * NTB * TB * shape[1] * KS * LB, NTB * TB * (shape[1] + 256) * 2 + shape[0] * shape[1] * 2),
        name="dec_grad",
    )(meta, *args)


def enc_grad_kernel(meta, cap, *refs):
    out, acc = refs[-2:]
    acc[...] = jnp.zeros_like(acc)
    for g in range(GROUPS):
        mine, other = refs[2 * g : 2 * g + 2]

        def body(b, carry):
            gid = g * NB + b
            ia, ib = pair_of(meta, gid)
            grads = jnp.concatenate([mine[rows_of(b), :], other[rows_of(b), :]], axis=1)
            prod = lax.dot_general(
                cap[rows_of(gid), :], grads, (((0,), (0,)), ((), ())), preferred_element_type=F32
            )
            acc[ia] += prod[:, :LB]
            acc[ib] += prod[:, LB:]
            return carry

        lax.fori_loop(0, NB, body, 0, unroll=2)
    for i in range(acc.shape[0]):
        out[:, i * LB : (i + 1) * LB] = acc[i].astype(BF)


def make_enc_grad(meta, captured, shape, groups):
    args = [a for pair in groups for a in pair]
    return pl.pallas_call(
        enc_grad_kernel,
        in_specs=[SMEM] + [VMEM] * (1 + len(args)),
        out_specs=VMEM,
        out_shape=jax.ShapeDtypeStruct(shape, BF),
        scratch_shapes=[pltpu.VMEM((shape[1] // LB, shape[0], LB), F32)],
        compiler_params=params(),
        cost_estimate=cost(2 * NTB * TB * shape[0] * KS * LB, NTB * TB * (shape[0] + 256) * 2 + shape[0] * shape[1] * 2),
        name="enc_grad",
    )(meta, captured, *args)


def tok_scatter(mine, theirs):
    got = lax.ppermute(theirs, "core", SWAP)
    pair = (mine.astype(F32) + got.astype(F32)).astype(BF)
    return lax.all_to_all(pair.reshape(CHIPS, BPC * TB, LB), ("y", "x"), 0, 0, tiled=True)


def tok_gather(copies):
    mine = lax.all_to_all(copies, ("y", "x"), 0, 0, tiled=True).reshape(NB * TB, LB)
    return mine, lax.ppermute(mine, "core", SWAP)


def local(captured, enc_weight, enc_bias, dec_weight, dec_bias, block_ids, block_counts):
    chip = lax.axis_index(("y", "x"))
    place = jnp.stack([lax.axis_index("core"), chip, lax.axis_index("lat")]).astype(jnp.int32)
    meta = jnp.concatenate([block_ids.reshape(-1), block_counts.reshape(-1), place])
    enc_bias = enc_bias.reshape(-1, LB)
    dec_bias = dec_bias.reshape(1, -1)

    codes, deltas, dpres = [], [], []
    for g in range(GROUPS):
        terms = tok_scatter(*encode(g, meta, captured, enc_weight))
        copies, own = make_codes(g, meta, terms, enc_bias)
        mine, other = tok_gather(copies)
        pieces = make_parts(g, meta, mine, other, dec_weight)
        delta = reduce_z(g, meta, pieces, dec_bias, captured)
        deltas.append(gather_z(delta))
        codes.append((mine, other))
        terms = tok_scatter(*make_dcodes(g, meta, dec_weight, deltas[g]))
        dpres.append(tok_gather(make_dpre(terms, own)))
    dec_grad = make_dec_grad(meta, dec_weight.shape, [(*codes[g], deltas[g]) for g in range(GROUPS)])
    enc_grad = make_enc_grad(meta, captured, enc_weight.shape, dpres)
    return enc_grad, dec_grad


def solution(mesh):
    cube = Mesh(mesh.devices.reshape(NY, NX, NC, NZ), ("y", "x", "core", "lat"))
    tok = ("y", "x", "core")
    in_specs = (
        P(None, tok),
        P(tok, "lat"),
        P("lat"),
        P("lat", tok),
        P(tok),
        P(None, "lat", None),
        P(None, "lat"),
    )
    out_specs = (P(tok, "lat"), P("lat", tok))
    return jax.shard_map(local, mesh=cube, in_specs=in_specs, out_specs=out_specs, check_vma=False)
```

time: 484 us -> 226 us (0.47)
  waiting for transfers between devices: 334 us -> 77.4 us
  blocking collectives: 0 us -> 81.6 us
  matrix products: 61 us -> 0 us
  local copies, waits for them, and re-layouts: 65.5 us -> 5.43 us
  starting transfers between devices: 0.34 us -> 29.1 us
  Pallas kernels: 0 us -> 27.2 us
  between operations: 13.9 us -> 0.77 us
  other arithmetic: 8.29 us -> 0.55 us
    psum x2 -> x0, waiting for transfers between devices: 203 us -> none  [the longest x1 104 us: local(): lax.psum(partial_value.reshape(all_blocks * TB, features).astype(jnp.bflo...]
    reduce_scatter x1 -> x0, waiting for transfers between devices: 87.1 us -> none  [local(): lax.psum_scatter(jnp.einsum('btf,fbkc->bktc', block_rows, weight_tiles, p...]
    all_to_all x0 -> x4, blocking collectives: none -> 81.6 us  [the longest x2 42.4 us: tok_scatter(): lax.all_to_all(pair.reshape(CHIPS, BPC * TB, LB), ('y', 'x'), 0, 0, tiled...]
    ppermute x0 -> x20, waiting for transfers between devices: none -> 77.4 us  [the longest x8 69.1 us: to_right(): return lax.ppermute(x, 'lat', RIGHT)]
    dot_general x7 -> x0, matrix products: 61 us -> none  [the longest x1 12.1 us: local(): jnp.einsum('bkj,bkcf->jcf', selector, tile_grads, precision=lax.Precision...]
    all_gather x1 -> x0, waiting for transfers between devices: 43.9 us -> none  [local(): codes_all = lax.all_gather(codes_own, 'tok', axis=0, tiled=True)]
    ppermute x0 -> x20, starting transfers between devices: none -> 29.1 us  [the longest x8 20.3 us: to_left(): return lax.ppermute(x, 'lat', LEFT)]
    pallas_call x0 -> x11, Pallas kernels: none -> 27.2 us  [the longest x1 9.1 us: make_enc_grad(): pl.pallas_call(enc_grad_kernel, in_specs=[SMEM] + [VMEM] * (1 + len(args)...]
  transfers between devices with their start and end apart: 4 -> 20, of which waited for: 4 -> 12; matrix products, arithmetic and copies ran while one was open for 6% -> 0% of each run, Pallas kernels for 0% -> 2%
where the time goes in v1:
time: 226 us; the launch traced here: 222 us
  blocking collectives  81.6 us (36%)
  waiting for transfers between devices  77.4 us (34%)
  starting transfers between devices  29.1 us (13%)
  Pallas kernels  27.2 us (12%)
  local copies, waits for them, and re-layouts  5.43 us (2%)
    ppermute x8, waiting for transfers between devices, to_right(): return lax.ppermute(x, 'lat', RIGHT)  69.1 us
    all_to_all x2, blocking collectives, tok_scatter(): lax.all_to_all(pair.reshape(CHIPS, BPC * TB, LB), ('y', 'x'), 0, 0, tiled...  42.4 us
    all_to_all x2, blocking collectives, tok_gather(): lax.all_to_all(copies, ('y', 'x'), 0, 0, tiled=True).reshape(NB * TB, LB)  39.2 us
    ppermute x8, starting transfers between devices, to_left(): return lax.ppermute(x, 'lat', LEFT)  20.3 us
    pallas_call x1, Pallas kernels, make_enc_grad(): pl.pallas_call(enc_grad_kernel, in_specs=[SMEM] + [VMEM] * (1 + len(args)...  9.1 us
    ppermute x8, starting transfers between devices, to_right(): return lax.ppermute(x, 'lat', RIGHT)  8.59 us
    pallas_call x1, Pallas kernels, encode(): pl.pallas_call(functools.partial(enc_kernel, group * NB, sb), grid=(steps...  5.69 us
    ppermute x2, waiting for transfers between devices, tok_scatter(): got = lax.ppermute(theirs, 'core', SWAP)  5.29 us
  transfers between devices with their start and end apart: 20, of which 12 were waited for; matrix products, arithmetic and copies ran while one was open for 0% of the time, Pallas kernels for 2%

profile of v1, /device:TPU:6, one launch (start us, length us, event | category | flops | bytes accessed | tf_op | source)
XLA Modules:
  0.0 222.1 jit_solution(17002453776922278078)
XLA Ops:
  0.6 0.8 copy.10
  1.5 0.7 concatenate.3.meta
  2.2 2.2 copy-done
  4.4 1.6 copy-done.3
  6.0 5.7 %encode.1 = (bf16[4096,128]{1,0:T(8,128)(2,1)S(1)}, bf16[4096,128]{1,0:T(8,128)(2,1)S(1)}) custom-call(s32[99]{0:T(128)S(1)} %concatenate.3.meta, bf16[4096,512]{1,0:T(8,128)(2,1)S(1)} %copy-done, bf16[512,2048]{1,0:T(8,128)(2,1)S(1)} %copy-done.3), custom_call_target="tpu_custom_call" | custom-call | flops 1073741824 | bytes 8388608 | tf_op jit(solution)/shard_map/encode/pallas_call | solution.py:72
  11.8 2.6 %collective-permute-done = bf16[4096,128]{1,0:T(8,128)(2,1)S(1)} collective-permute-done((bf16[4096,128]{1,0:T(8,128)(2,1)S(1)}, bf16[4096,128]{1,0:T(8,128)(2,1)S(1)}, u32[]{:S(2)}, u32[]{:S(2)}) %collective-permute-start) | collective-permute-done | bytes 1048608 | tf_op jit(solution)/shard_map/ppermute | solution.py:366
  14.5 0.3 add_convert_fusion.1
  14.8 22.0 %all_to_all.20.terms = bf16[16,256,128]{2,1,0:T(8,128)(2,1)S(1)} all-to-all(bf16[16,256,128]{2,1,0:T(8,128)(2,1)S(1)} %bitcast.19), channel_id=1, replica_groups=mesh['y'=4,'x'=4,'core'=2,'lat'=8] {'y','x'}, dimensions={0} | all-to-all | bytes 2097152 | tf_op jit(solution)/shard_map/all_to_all | solution.py:368
  36.8 0.8 codes.1
  37.6 19.6 %all_to_all.21 = bf16[16,256,128]{2,1,0:T(8,128)(2,1)S(1)} all-to-all(bf16[16,256,128]{2,1,0:T(8,128)(2,1)S(1)} %get-tuple-element.25), channel_id=1, replica_groups=mesh['y'=4,'x'=4,'core'=2,'lat'=8] {'y','x'}, dimensions={0} | all-to-all | bytes 2097152 | tf_op jit(solution)/shard_map/all_to_all | solution.py:372
  57.2 2.7 %collective-permute-done.1.other.refs_1_ = bf16[4096,128]{1,0:T(8,128)(2,1)S(1)} collective-permute-done((bf16[4096,128]{1,0:T(8,128)(2,1)S(1)}, bf16[4096,128]{1,0:T(8,128)(2,1)S(1)}, u32[]{:S(2)}, u32[]{:S(2)}) %collective-permute-start.1) | collective-permute-done | bytes 1048608 | tf_op jit(solution)/shard_map/ppermute | solution.py:373
  59.9 1.8 parts.1
  61.7 2.0 collective-permute-start.2
  63.7 4.0 %collective-permute-start.3 = (bf16[256,512]{1,0:T(8,128)(2,1)S(1)}, bf16[256,512]{1,0:T(8,128)(2,1)S(1)}, u32[]{:S(2)}, u32[]{:S(2)}) collective-permute-start(bf16[256,512]{1,0:T(8,128)(2,1)S(1)} %get-tuple-element.32), channel_id=1, source_target_pairs={{0,7},{1,0},{2,1},{3,2},{4,3},{5,4},{6,5},{7,6},{8,15},{9,8},{10,9... | collective-permute-start | bytes 786440 | tf_op jit(solution)/shard_map/ppermute | solution.py:241
  67.7 6.5 %collective-permute-done.2.ra = bf16[256,512]{1,0:T(8,128)(2,1)S(1)} collective-permute-done((bf16[256,512]{1,0:T(8,128)(2,1)S(1)}, bf16[256,512]{1,0:T(8,128)(2,1)S(1)}, u32[]{:S(2)}, u32[]{:S(2)}) %collective-permute-start.2) | collective-permute-done | bytes 262176 | tf_op jit(solution)/shard_map/ppermute | solution.py:237
  74.3 0.1 ring_add.3
  74.5 3.2 %collective-permute-start.5 = (bf16[512,512]{1,0:T(8,128)(2,1)S(1)}, bf16[512,512]{1,0:T(8,128)(2,1)S(1)}, u32[]{:S(2)}, u32[]{:S(2)}) collective-permute-start(bf16[512,512]{1,0:T(8,128)(2,1)S(1)} %get-tuple-element.35), channel_id=1, source_target_pairs={{0,7},{1,0},{2,1},{3,2},{4,3},{5,4},{6,5},{7,6},{8,15},{9,8},{10,9... | collective-permute-start | bytes 1572872 | tf_op jit(solution)/shard_map/ppermute | solution.py:241
  77.7 11.4 %collective-permute-done.4.refs_1_ = bf16[512,512]{1,0:T(8,128)(2,1)S(1)} collective-permute-done((bf16[512,512]{1,0:T(8,128)(2,1)S(1)}, bf16[512,512]{1,0:T(8,128)(2,1)S(1)}, u32[]{:S(2)}, u32[]{:S(2)}) %collective-permute-start.4) | collective-permute-done | bytes 524320 | tf_op jit(solution)/shard_map/ppermute | solution.py:237
  89.2 0.3 ring_add.4
  89.4 1.9 collective-permute-start.6
  91.3 1.4 collective-permute-start.7
  92.7 10.5 %collective-permute-done.6.refs_1_ = bf16[512,512]{1,0:T(8,128)(2,1)S(1)} collective-permute-done((bf16[512,512]{1,0:T(8,128)(2,1)S(1)}, bf16[512,512]{1,0:T(8,128)(2,1)S(1)}, u32[]{:S(2)}, u32[]{:S(2)}) %collective-permute-start.6) | collective-permute-done | bytes 524320 | tf_op jit(solution)/shard_map/ppermute | solution.py:237
  103.3 0.2 ring_add.5
  103.5 1.6 collective-permute-start.8
  105.1 1.7 collective-permute-start.9
  106.8 9.6 %collective-permute-done.8.ra = bf16[512,512]{1,0:T(8,128)(2,1)S(1)} collective-permute-done((bf16[512,512]{1,0:T(8,128)(2,1)S(1)}, bf16[512,512]{1,0:T(8,128)(2,1)S(1)}, u32[]{:S(2)}, u32[]{:S(2)}) %collective-permute-start.8) | collective-permute-done | bytes 524320 | tf_op jit(solution)/shard_map/ppermute | solution.py:237
  116.4 0.9 delta.1.refs_0_.refs_2_
  117.3 1.2 collective-permute-start.11
  118.5 2.1 collective-permute-start.10
  120.6 8.8 %collective-permute-done.11.refs_2_.refs_4_ = bf16[512,512]{1,0:T(8,128)(2,1)S(1)} collective-permute-done((bf16[512,512]{1,0:T(8,128)(2,1)S(1)}, bf16[512,512]{1,0:T(8,128)(2,1)S(1)}, u32[]{:S(2)}, u32[]{:S(2)}) %collective-permute-start.11) | collective-permute-done | bytes 524320 | tf_op jit(solution)/shard_map/ppermute | solution.py:237
  129.5 0.4 collective-permute-start.13
  129.9 2.8 %collective-permute-start.12 = (bf16[512,512]{1,0:T(8,128)(2,1)S(1)}, bf16[512,512]{1,0:T(8,128)(2,1)S(1)}, u32[]{:S(2)}, u32[]{:S(2)}) collective-permute-start(bf16[512,512]{1,0:T(8,128)(2,1)S(1)} %collective-permute-done.10.refs_1_.refs_3_), channel_id=1, source_target_pairs={{0,7},{1,0},{2,1},{3,2},{4,3},{5,4},{6,5},{7,6},{8,15},{9,8},{10,9... | collective-permute-start | bytes 1572872 | tf_op jit(solution)/shard_map/ppermute | solution.py:241
  132.7 8.8 %collective-permute-done.13.refs_4_.refs_6_ = bf16[512,512]{1,0:T(8,128)(2,1)S(1)} collective-permute-done((bf16[512,512]{1,0:T(8,128)(2,1)S(1)}, bf16[512,512]{1,0:T(8,128)(2,1)S(1)}, u32[]{:S(2)}, u32[]{:S(2)}) %collective-permute-start.13) | collective-permute-done | bytes 524320 | tf_op jit(solution)/shard_map/ppermute | solution.py:237
  141.6 0.9 collective-permute-start.15
  142.4 2.4 %collective-permute-start.14 = (bf16[512,512]{1,0:T(8,128)(2,1)S(1)}, bf16[512,512]{1,0:T(8,128)(2,1)S(1)}, u32[]{:S(2)}, u32[]{:S(2)}) collective-permute-start(bf16[512,512]{1,0:T(8,128)(2,1)S(1)} %collective-permute-done.12.refs_3_.refs_5_), channel_id=1, source_target_pairs={{0,7},{1,0},{2,1},{3,2},{4,3},{5,4},{6,5},{7,6},{8,15},{9,8},{10,9... | collective-permute-start | bytes 1572872 | tf_op jit(solution)/shard_map/ppermute | solution.py:241
  144.8 9.2 %collective-permute-done.15.refs_6_.refs_8_ = bf16[512,512]{1,0:T(8,128)(2,1)S(1)} collective-permute-done((bf16[512,512]{1,0:T(8,128)(2,1)S(1)}, bf16[512,512]{1,0:T(8,128)(2,1)S(1)}, u32[]{:S(2)}, u32[]{:S(2)}) %collective-permute-start.15) | collective-permute-done | bytes 524320 | tf_op jit(solution)/shard_map/ppermute | solution.py:237
  154.0 0.5 collective-permute-start.16
  154.5 0.4 collective-permute-done.14.refs_5_.refs_7_
  154.9 2.6 %collective-permute-start.17 = (bf16[256,512]{1,0:T(8,128)(2,1)S(1)}, bf16[256,512]{1,0:T(8,128)(2,1)S(1)}, u32[]{:S(2)}, u32[]{:S(2)}) collective-permute-start(bf16[256,512]{1,0:T(8,128)(2,1)S(1)} %slice.9), channel_id=1, source_target_pairs={{0,7},{1,0},{2,1},{3,2},{4,3},{5,4},{6,5},{7,6},{8,15},{9,8},{10,9... | collective-permute-start | bytes 786440 | tf_op jit(solution)/shard_map/ppermute | solution.py:241
  157.5 4.2 %collective-permute-done.16.refs_7_.refs_9_ = bf16[256,512]{1,0:T(8,128)(2,1)S(1)} collective-permute-done((bf16[256,512]{1,0:T(8,128)(2,1)S(1)}, bf16[256,512]{1,0:T(8,128)(2,1)S(1)}, u32[]{:S(2)}, u32[]{:S(2)}) %collective-permute-start.16) | collective-permute-done | bytes 262176 | tf_op jit(solution)/shard_map/ppermute | solution.py:237
  161.7 3.4 %dcodes.1 = (bf16[4096,128]{1,0:T(8,128)(2,1)S(1)}, bf16[4096,128]{1,0:T(8,128)(2,1)S(1)}) custom-call(s32[99]{0:T(128)S(1)} %concatenate.3.meta, bf16[2048,512]{1,0:T(8,128)(2,1)S(1)} %copy-done.2, bf16[512,512]{1,0:T(8,128)(2,1)S(1)} %delta.1.refs_0_.refs_2_, bf16[512,512]{1,0:T(8,128)(2,1)S(1)} %collective-permute-done.10.refs_1_.refs_3_, ...), custom_call_target="tpu_custom_call" | custom-call | flops 1073741824 | bytes 8388608 | tf_op jit(solution)/shard_map/dcodes/pallas_call | solution.py:283
  165.2 2.6 %collective-permute-done.18 = bf16[4096,128]{1,0:T(8,128)(2,1)S(1)} collective-permute-done((bf16[4096,128]{1,0:T(8,128)(2,1)S(1)}, bf16[4096,128]{1,0:T(8,128)(2,1)S(1)}, u32[]{:S(2)}, u32[]{:S(2)}) %collective-permute-start.18) | collective-permute-done | bytes 1048608 | tf_op jit(solution)/shard_map/ppermute | solution.py:366
  167.8 0.3 add_convert_fusion
  168.1 20.4 %all_to_all.22.terms = bf16[16,256,128]{2,1,0:T(8,128)(2,1)S(1)} all-to-all(bf16[16,256,128]{2,1,0:T(8,128)(2,1)S(1)} %bitcast.20), channel_id=1, replica_groups=mesh['y'=4,'x'=4,'core'=2,'lat'=8] {'y','x'}, dimensions={0} | all-to-all | bytes 2097152 | tf_op jit(solution)/shard_map/all_to_all | solution.py:368
  188.5 0.2 dpre.1
  188.7 19.6 %all_to_all.23 = bf16[16,256,128]{2,1,0:T(8,128)(2,1)S(1)} all-to-all(bf16[16,256,128]{2,1,0:T(8,128)(2,1)S(1)} %dpre.1), channel_id=1, replica_groups=mesh['y'=4,'x'=4,'core'=2,'lat'=8] {'y','x'}, dimensions={0} | all-to-all | bytes 2097152 | tf_op jit(solution)/shard_map/all_to_all | solution.py:372
  208.3 4.7 %dec_grad.1 = bf16[2048,512]{1,0:T(8,128)(2,1)} custom-call(s32[99]{0:T(128)S(1)} %concatenate.3.meta, bf16[4096,128]{1,0:T(8,128)(2,1)S(1)} %bitcast.14, bf16[4096,128]{1,0:T(8,128)(2,1)S(1)} %collective-permute-done.1.other.refs_1_, bf16[512,512]{1,0:T(8,128)(2,1)S(1)} %delta.1.refs_0_.refs_2_, ...), custom_call_target="tpu_custom_call" | custom-call | flops 1073741824 | bytes 8388608 | tf_op jit(solution)/shard_map/dec_grad/pallas_call | solution.py:317
  213.0 9.1 %enc_grad.1 = bf16[512,2048]{1,0:T(8,128)(2,1)} custom-call(s32[99]{0:T(128)S(1)} %concatenate.3.meta, bf16[4096,512]{1,0:T(8,128)(2,1)S(1)} %copy-done.1, bf16[4096,128]{1,0:T(8,128)(2,1)S(1)} %bitcast.16, bf16[4096,128]{1,0:T(8,128)(2,1)S(1)} %collective-permute-done.19.refs_1_), custom_call_target="tpu_custom_call" | custom-call | flops 1073741824 | bytes 8388608 | tf_op jit(solution)/shard_map/enc_grad/pallas_call | solution.py:353
  (26 shorter events, 0.5 us)
Async XLA Ops:
  2.2 2.2 copy-start
  4.4 1.6 copy-start.3
  11.7 2.7 %collective-permute-start = (bf16[4096,128]{1,0:T(8,128)(2,1)S(1)}, bf16[4096,128]{1,0:T(8,128)(2,1)S(1)}, u32[]{:S(2)}, u32[]{:S(2)}) collective-permute-start(bf16[4096,128]{1,0:T(8,128)(2,1)S(1)} %get-tuple-element.24), channel_id=1, source_target_pairs={{0,8},{8,0},{1,9},{9,1},{2,10},{10,2},{3,11},{11,3},{4,12},{12,4},... | collective-permute-start | bytes 3145736 | tf_op jit(solution)/shard_map/ppermute | solution.py:366
  14.5 22.3 %copy-start.4 = (f32[2048]{0:T(1024)S(1)}, f32[2048]{0:T(1024)}, u32[]{:S(2)}) copy-start(f32[2048]{0:T(1024)} %param.9) | copy-start | bytes 24580
  36.8 23.1 %copy-start.2 = (bf16[2048,512]{1,0:T(8,128)(2,1)S(1)}, bf16[2048,512]{1,0:T(8,128)(2,1)}, u32[]{:S(2)}) copy-start(bf16[2048,512]{1,0:T(8,128)(2,1)} %dec.3) | copy-start | bytes 6291460
  57.2 2.7 %collective-permute-start.1 = (bf16[4096,128]{1,0:T(8,128)(2,1)S(1)}, bf16[4096,128]{1,0:T(8,128)(2,1)S(1)}, u32[]{:S(2)}, u32[]{:S(2)}) collective-permute-start(bf16[4096,128]{1,0:T(8,128)(2,1)S(1)} %bitcast.12), channel_id=1, source_target_pairs={{0,8},{8,0},{1,9},{9,1},{2,10},{10,2},{3,11},{11,3},{4,12},{12,4},... | collective-permute-start | bytes 3145736 | tf_op jit(solution)/shard_map/ppermute | solution.py:373
  61.7 12.5 %collective-permute-start.2 = (bf16[256,512]{1,0:T(8,128)(2,1)S(1)}, bf16[256,512]{1,0:T(8,128)(2,1)S(1)}, u32[]{:S(2)}, u32[]{:S(2)}) collective-permute-start(bf16[256,512]{1,0:T(8,128)(2,1)S(1)} %get-tuple-element.30), channel_id=1, source_target_pairs={{0,1},{1,2},{2,3},{3,4},{4,5},{5,6},{6,7},{7,0},{8,9},{9,10},{10,1... | collective-permute-start | bytes 786440 | tf_op jit(solution)/shard_map/ppermute | solution.py:237
  63.7 10.6 %collective-permute-start.3 = (bf16[256,512]{1,0:T(8,128)(2,1)S(1)}, bf16[256,512]{1,0:T(8,128)(2,1)S(1)}, u32[]{:S(2)}, u32[]{:S(2)}) collective-permute-start(bf16[256,512]{1,0:T(8,128)(2,1)S(1)} %get-tuple-element.32), channel_id=1, source_target_pairs={{0,7},{1,0},{2,1},{3,2},{4,3},{5,4},{6,5},{7,6},{8,15},{9,8},{10,9... | collective-permute-start | bytes 786440 | tf_op jit(solution)/shard_map/ppermute | solution.py:241
  74.4 14.7 %collective-permute-start.4 = (bf16[512,512]{1,0:T(8,128)(2,1)S(1)}, bf16[512,512]{1,0:T(8,128)(2,1)S(1)}, u32[]{:S(2)}, u32[]{:S(2)}) collective-permute-start(bf16[512,512]{1,0:T(8,128)(2,1)S(1)} %get-tuple-element.33), channel_id=1, source_target_pairs={{0,1},{1,2},{2,3},{3,4},{4,5},{5,6},{6,7},{7,0},{8,9},{9,10},{10,1... | collective-permute-start | bytes 1572872 | tf_op jit(solution)/shard_map/ppermute | solution.py:237
  74.5 14.7 %collective-permute-start.5 = (bf16[512,512]{1,0:T(8,128)(2,1)S(1)}, bf16[512,512]{1,0:T(8,128)(2,1)S(1)}, u32[]{:S(2)}, u32[]{:S(2)}) collective-permute-start(bf16[512,512]{1,0:T(8,128)(2,1)S(1)} %get-tuple-element.35), channel_id=1, source_target_pairs={{0,7},{1,0},{2,1},{3,2},{4,3},{5,4},{6,5},{7,6},{8,15},{9,8},{10,9... | collective-permute-start | bytes 1572872 | tf_op jit(solution)/shard_map/ppermute | solution.py:241
  89.1 27.3 %copy-start.1 = (bf16[4096,512]{1,0:T(8,128)(2,1)S(1)}, bf16[4096,512]{1,0:T(8,128)(2,1)}, u32[]{:S(2)}) copy-start(bf16[4096,512]{1,0:T(8,128)(2,1)} %cap.5) | copy-start | bytes 12582916
  89.2 27.3 %copy-start.5 = (f32[512]{0:T(512)S(1)}, f32[512]{0:T(512)}, u32[]{:S(2)}) copy-start(f32[512]{0:T(512)} %param.11) | copy-start | bytes 6148
  89.4 13.8 %collective-permute-start.6 = (bf16[512,512]{1,0:T(8,128)(2,1)S(1)}, bf16[512,512]{1,0:T(8,128)(2,1)S(1)}, u32[]{:S(2)}, u32[]{:S(2)}) collective-permute-start(bf16[512,512]{1,0:T(8,128)(2,1)S(1)} %get-tuple-element.36), channel_id=1, source_target_pairs={{0,1},{1,2},{2,3},{3,4},{4,5},{5,6},{6,7},{7,0},{8,9},{9,10},{10,1... | collective-permute-start | bytes 1572872 | tf_op jit(solution)/shard_map/ppermute | solution.py:237
  91.3 12.0 %collective-permute-start.7 = (bf16[512,512]{1,0:T(8,128)(2,1)S(1)}, bf16[512,512]{1,0:T(8,128)(2,1)S(1)}, u32[]{:S(2)}, u32[]{:S(2)}) collective-permute-start(bf16[512,512]{1,0:T(8,128)(2,1)S(1)} %get-tuple-element.38), channel_id=1, source_target_pairs={{0,7},{1,0},{2,1},{3,2},{4,3},{5,4},{6,5},{7,6},{8,15},{9,8},{10,9... | collective-permute-start | bytes 1572872 | tf_op jit(solution)/shard_map/ppermute | solution.py:241
  103.5 12.9 %collective-permute-start.8 = (bf16[512,512]{1,0:T(8,128)(2,1)S(1)}, bf16[512,512]{1,0:T(8,128)(2,1)S(1)}, u32[]{:S(2)}, u32[]{:S(2)}) collective-permute-start(bf16[512,512]{1,0:T(8,128)(2,1)S(1)} %get-tuple-element.39), channel_id=1, source_target_pairs={{0,1},{1,2},{2,3},{3,4},{4,5},{5,6},{6,7},{7,0},{8,9},{9,10},{10,1... | collective-permute-start | bytes 1572872 | tf_op jit(solution)/shard_map/ppermute | solution.py:237
  105.1 11.3 %collective-permute-start.9 = (bf16[512,512]{1,0:T(8,128)(2,1)S(1)}, bf16[512,512]{1,0:T(8,128)(2,1)S(1)}, u32[]{:S(2)}, u32[]{:S(2)}) collective-permute-start(bf16[512,512]{1,0:T(8,128)(2,1)S(1)} %get-tuple-element.40), channel_id=1, source_target_pairs={{0,7},{1,0},{2,1},{3,2},{4,3},{5,4},{6,5},{7,6},{8,15},{9,8},{10,9... | collective-permute-start | bytes 1572872 | tf_op jit(solution)/shard_map/ppermute | solution.py:241
  117.3 12.2 %collective-permute-start.11 = (bf16[512,512]{1,0:T(8,128)(2,1)S(1)}, bf16[512,512]{1,0:T(8,128)(2,1)S(1)}, u32[]{:S(2)}, u32[]{:S(2)}) collective-permute-start(bf16[512,512]{1,0:T(8,128)(2,1)S(1)} %delta.1.refs_0_.refs_2_), channel_id=1, source_target_pairs={{0,1},{1,2},{2,3},{3,4},{4,5},{5,6},{6,7},{7,0},{8,9},{9,10},{10,1... | collective-permute-start | bytes 1572872 | tf_op jit(solution)/shard_map/ppermute | solution.py:237
  118.5 11.4 %collective-permute-start.10 = (bf16[512,512]{1,0:T(8,128)(2,1)S(1)}, bf16[512,512]{1,0:T(8,128)(2,1)S(1)}, u32[]{:S(2)}, u32[]{:S(2)}) collective-permute-start(bf16[512,512]{1,0:T(8,128)(2,1)S(1)} %delta.1.refs_0_.refs_2_), channel_id=1, source_target_pairs={{0,7},{1,0},{2,1},{3,2},{4,3},{5,4},{6,5},{7,6},{8,15},{9,8},{10,9... | collective-permute-start | bytes 1572872 | tf_op jit(solution)/shard_map/ppermute | solution.py:241
  129.5 12.1 %collective-permute-start.13 = (bf16[512,512]{1,0:T(8,128)(2,1)S(1)}, bf16[512,512]{1,0:T(8,128)(2,1)S(1)}, u32[]{:S(2)}, u32[]{:S(2)}) collective-permute-start(bf16[512,512]{1,0:T(8,128)(2,1)S(1)} %collective-permute-done.11.refs_2_.refs_4_), channel_id=1, source_target_pairs={{0,1},{1,2},{2,3},{3,4},{4,5},{5,6},{6,7},{7,0},{8,9},{9,10},{10,1... | collective-permute-start | bytes 1572872 | tf_op jit(solution)/shard_map/ppermute | solution.py:237
  129.9 12.5 %collective-permute-start.12 = (bf16[512,512]{1,0:T(8,128)(2,1)S(1)}, bf16[512,512]{1,0:T(8,128)(2,1)S(1)}, u32[]{:S(2)}, u32[]{:S(2)}) collective-permute-start(bf16[512,512]{1,0:T(8,128)(2,1)S(1)} %collective-permute-done.10.refs_1_.refs_3_), channel_id=1, source_target_pairs={{0,7},{1,0},{2,1},{3,2},{4,3},{5,4},{6,5},{7,6},{8,15},{9,8},{10,9... | collective-permute-start | bytes 1572872 | tf_op jit(solution)/shard_map/ppermute | solution.py:241
  141.6 12.4 %collective-permute-start.15 = (bf16[512,512]{1,0:T(8,128)(2,1)S(1)}, bf16[512,512]{1,0:T(8,128)(2,1)S(1)}, u32[]{:S(2)}, u32[]{:S(2)}) collective-permute-start(bf16[512,512]{1,0:T(8,128)(2,1)S(1)} %collective-permute-done.13.refs_4_.refs_6_), channel_id=1, source_target_pairs={{0,1},{1,2},{2,3},{3,4},{4,5},{5,6},{6,7},{7,0},{8,9},{9,10},{10,1... | collective-permute-start | bytes 1572872 | tf_op jit(solution)/shard_map/ppermute | solution.py:237
  142.4 12.4 %collective-permute-start.14 = (bf16[512,512]{1,0:T(8,128)(2,1)S(1)}, bf16[512,512]{1,0:T(8,128)(2,1)S(1)}, u32[]{:S(2)}, u32[]{:S(2)}) collective-permute-start(bf16[512,512]{1,0:T(8,128)(2,1)S(1)} %collective-permute-done.12.refs_3_.refs_5_), channel_id=1, source_target_pairs={{0,7},{1,0},{2,1},{3,2},{4,3},{5,4},{6,5},{7,6},{8,15},{9,8},{10,9... | collective-permute-start | bytes 1572872 | tf_op jit(solution)/shard_map/ppermute | solution.py:241
  154.0 7.7 %collective-permute-start.16 = (bf16[256,512]{1,0:T(8,128)(2,1)S(1)}, bf16[256,512]{1,0:T(8,128)(2,1)S(1)}, u32[]{:S(2)}, u32[]{:S(2)}) collective-permute-start(bf16[256,512]{1,0:T(8,128)(2,1)S(1)} %slice.8), channel_id=1, source_target_pairs={{0,1},{1,2},{2,3},{3,4},{4,5},{5,6},{6,7},{7,0},{8,9},{9,10},{10,1... | collective-permute-start | bytes 786440 | tf_op jit(solution)/shard_map/ppermute | solution.py:237
  154.9 6.7 %collective-permute-start.17 = (bf16[256,512]{1,0:T(8,128)(2,1)S(1)}, bf16[256,512]{1,0:T(8,128)(2,1)S(1)}, u32[]{:S(2)}, u32[]{:S(2)}) collective-permute-start(bf16[256,512]{1,0:T(8,128)(2,1)S(1)} %slice.9), channel_id=1, source_target_pairs={{0,7},{1,0},{2,1},{3,2},{4,3},{5,4},{6,5},{7,6},{8,15},{9,8},{10,9... | collective-permute-start | bytes 786440 | tf_op jit(solution)/shard_map/ppermute | solution.py:241
  165.1 2.7 %collective-permute-start.18 = (bf16[4096,128]{1,0:T(8,128)(2,1)S(1)}, bf16[4096,128]{1,0:T(8,128)(2,1)S(1)}, u32[]{:S(2)}, u32[]{:S(2)}) collective-permute-start(bf16[4096,128]{1,0:T(8,128)(2,1)S(1)} %get-tuple-element.42), channel_id=1, source_target_pairs={{0,8},{8,0},{1,9},{9,1},{2,10},{10,2},{3,11},{11,3},{4,12},{12,4},... | collective-permute-start | bytes 3145736 | tf_op jit(solution)/shard_map/ppermute | solution.py:366
  208.3 4.7 %collective-permute-start.19 = (bf16[4096,128]{1,0:T(8,128)(2,1)S(1)}, bf16[4096,128]{1,0:T(8,128)(2,1)S(1)}, u32[]{:S(2)}, u32[]{:S(2)}) collective-permute-start(bf16[4096,128]{1,0:T(8,128)(2,1)S(1)} %bitcast.15), channel_id=1, source_target_pairs={{0,8},{8,0},{1,9},{9,1},{2,10},{10,2},{3,11},{11,3},{4,12},{12,4},... | collective-permute-start | bytes 3145736 | tf_op jit(solution)/shard_map/ppermute | solution.py:373
